TPU v7x, 128 devices: a whole 4x4x4 slice. The times are simulated.
128 devices in a mesh: pipe: 2 (over y_hi), section: 8 (over x, y_lo), tp: 8 (over z, core).
Axes of the slice: x: 4, y: 4 (y_hi: 2, y_lo: 2; y = y_hi * 2 + y_lo), z: 4, core: 2. Of those that a mesh axis runs over, the one named last changes fastest.
Arguments:
- acts: bfloat16 [2, 16, 1536, 8192], P('pipe', 'section', None, 'tp'), may hold values from -6 to 6
- kv_grads: bfloat16 [2, 16, 1536, 2048], P('pipe', 'section', None, 'tp'), may hold values from -0.15625 to 0.15625
- layer_section: int32 [2, 12], replicated, may hold values from 0 to 7, as said below
- token_counts: int32 [2], replicated, may hold values from 768 to 1536, as said below
Outputs:
- summed_grads: bfloat16 [16, 8192, 2048], P('section', 'tp', 'pipe')
Inputs may be any that keep to these rules, and one draw needn't show every extreme that they name: `layer_section`: in each relay the section never falls as the layer index rises, every section holds 1 or 2 layers, sections 2 k and 2 k + 1 hold 3 layers together, and a layer's sections in the two relays differ by at most 1, by exactly 1 for some layer. `token_counts`: for one of the two relays it equals 1536.
All inputs are finite; a program needn't handle non-finite values.
Results may differ from a plain program's by a relative error of at most 0.0052.
Values may be sent and summed in bfloat16 or wider, within the bound.
No kernel may reach another device: no remote copies, remote signals or barrier semaphores. Data moves between devices by JAX's collectives and lax.ppermute only.
A program may use at most 128 MiB of HBM per device.

v0:
```python
import jax
import jax.numpy as jnp
from jax import lax
from jax.sharding import PartitionSpec as P


def from_behind(array, axis, by):
    size = lax.axis_size(axis)
    return lax.ppermute(array, axis, [(i, (i + by) % size) for i in range(size)])


def slot_table(section_row, section_total, slot_count):
    section_ids = jnp.arange(section_total, dtype=jnp.int32)
    first_layer = jnp.sum((section_row[None, :] < section_ids[:, None]).astype(jnp.int32), axis=1)
    layer_count = jnp.sum((section_row[None, :] == section_ids[:, None]).astype(jnp.int32), axis=1)
    offsets = jnp.arange(slot_count, dtype=jnp.int32)
    slot_layers = jnp.where(
        offsets[None, :] < layer_count[:, None], first_layer[:, None] + offsets[None, :], -1
    )
    return slot_layers.reshape(-1)


def shards(acts, kv_grads, layer_section, token_counts):
    section_total = lax.axis_size("section")
    pipe_id = lax.axis_index("pipe")
    section_id = lax.axis_index("section")
    slot_count = acts.shape[1]
    inputs = acts[0]
    kv_rows = kv_grads[0]
    token_limit = lax.dynamic_index_in_dim(token_counts, pipe_id, 0, keepdims=False)
    live_rows = jnp.arange(kv_rows.shape[1], dtype=jnp.int32) < token_limit
    kv_rows = jnp.where(live_rows[None, :, None], kv_rows, jnp.zeros_like(kv_rows))
    slot_tables = jnp.stack(
        [
            slot_table(layer_section[0], section_total, slot_count),
            slot_table(layer_section[1], section_total, slot_count),
        ]
    )
    own_table = lax.dynamic_index_in_dim(slot_tables, pipe_id, 0, keepdims=False)
    other_table = lax.dynamic_index_in_dim(slot_tables, 1 - pipe_id, 0, keepdims=False)
    my_layers = lax.dynamic_slice_in_dim(own_table, section_id * slot_count, slot_count)
    half_width = kv_rows.shape[2] * lax.axis_size("tp") // 2
    gradients = jnp.einsum(
        "std,stc->sdc",
        inputs,
        lax.all_gather(kv_rows, "tp", axis=2, tiled=True),
        preferred_element_type=jnp.float32,
    ).astype(jnp.bfloat16)
    own_part = lax.dynamic_slice_in_dim(gradients, pipe_id * half_width, half_width, 2)
    sent_part = lax.dynamic_slice_in_dim(gradients, (1 - pipe_id) * half_width, half_width, 2)
    own_part, sent_part = (own_part, sent_part)
    slot_ids = list(range(slot_count))
    partner_sum = jnp.zeros((slot_count, sent_part.shape[1], sent_part.shape[2]), jnp.float32)
    for offset in (-1, 0, 1):
        arrived = from_behind(sent_part, ("pipe", "section"), section_total + offset)
        source = section_id - offset
        inside = (source >= 0) & (source < section_total)
        source_clip = jnp.clip(source, 0, section_total - 1)
        slot_array = jnp.stack([jnp.asarray(value, dtype=jnp.int32) for value in slot_ids])
        layer_ids = jnp.take(other_table, source_clip * slot_count + slot_array)
        matches = (my_layers[:, None] == layer_ids[None, :]) & (my_layers[:, None] >= 0) & inside
        partner_sum = partner_sum + jnp.einsum(
            "jk,kdc->jdc", matches.astype(jnp.bfloat16), arrived, preferred_element_type=jnp.float32
        )
    summed = own_part.astype(jnp.float32) + partner_sum
    valid = (my_layers >= 0)[:, None, None]
    return jnp.where(valid, summed, jnp.zeros_like(summed)).astype(jnp.bfloat16)


def solution(mesh):
    placed = (P("pipe", "section", None, "tp"), P("pipe", "section", None, "tp"), P(), P())
    return jax.shard_map(
        shards, mesh=mesh, in_specs=placed, out_specs=P("section", "tp", "pipe"), check_vma=False
    )
```

profile of v0, /device:TPU:24, one launch (start us, length us, event | category | flops | bytes accessed | tf_op | source)
XLA Modules:
  0.0 504.4 jit_solution(16280116728958497793)
XLA Ops:
  6.5 0.0 all-gather.2.cloned.1.call-start
  6.5 1.2 dynamic_slice.22
  7.8 0.7 iota_compare_fusion
  8.4 1.7 copy.21
  10.2 1.3 bitcast_select_fusion
  11.4 0.0 all-gather.2.cloned.1.call-update
  11.4 69.8 %all-gather.2.cloned.1.call-done = bf16[2,1536,2048]{1,2,0:T(8,128)(2,1)} async-done(((bf16[2,1536,256]{1,2,0:T(8,128)(2,1)}), bf16[2,1536,2048]{1,2,0:T(8,128)(2,1)}) %all-gather.2.cloned.1.call-update) | async-done | bytes 12582928 | tf_op jit(solution)/shard_map/all_gather | solution.py:46
  81.2 17.7 %fusion.4 = bf16[2,2048,1024]{2,1,0:T(8,128)(2,1)S(1)} fusion(bf16[2,1536,2048]{1,2,0:T(8,128)(2,1)} %all-gather.2.cloned.1.call-done, bf16[1,2,1536,1024]{3,2,1,0:T(8,128)(2,1)} %param.6), kind=kOutput, calls=%fused_computation.8 | convolution fusion | flops 12889096192 | bytes 27262976 | tf_op jit(solution)/shard_map/std,stc->sdc/dot_general | solution.py:43
  98.9 0.0 copy-start
  98.9 3.2 copy-done
  102.1 0.0 copy-start.1
  102.1 2.5 dynamic-slice_bitcast_fusion
  104.6 1.4 collective-permute-start.2
  106.0 2.4 collective-permute-start.1
  108.4 0.2 collective-permute-start
  108.6 0.0 copy-done.1
  108.7 0.1 convert_reduce_fusion.1
  108.8 0.1 add_select_fusion
  108.9 0.1 select_n.67
  109.0 0.1 add_select_fusion.1
  109.0 0.1 select_n.65
  109.2 0.6 gather_fusion.2
  109.8 0.6 gather_fusion.1
  110.5 0.6 gather_fusion
  111.1 0.1 broadcast_compare_fusion
  111.2 267.4 %collective-permute-done.2 = bf16[2,1024,1024]{1,2,0:T(8,128)(2,1)} collective-permute-done((bf16[2,1024,1024]{1,2,0:T(8,128)(2,1)}, bf16[2,1024,1024]{1,2,0:T(8,128)(2,1)}, u32[]{:S(2)}, u32[]{:S(2)}) %collective-permute-start.2) | collective-permute-done | bytes 4194336 | tf_op jit(solution)/shard_map/ppermute | solution.py:9
  378.6 11.4 %copy.26 = bf16[2,1024,1024]{2,0,1:T(2,128)(2,1)} copy(bf16[2,1024,1024]{1,2,0:T(8,128)(2,1)} %collective-permute-done.2) | data formatting | bytes 8388608 | tf_op jit(solution)/shard_map/ppermute | solution.py:9
  390.0 8.7 %fusion.9 = f32[2,1024,1024]{2,0,1:T(2,128)} fusion(bf16[2,1024,1024]{2,0,1:T(2,128)(2,1)} %copy.26, pred[]{:T(512)S(6)} %and.63, pred[2]{0:T(512)(128)(4,1)S(1)} %get-tuple-element.10, s32[2]{0:T(128)S(1)} %and_select_fusion, s32[2]{0:T(128)S(1)} %get-tuple-element.11), kind=kOutput, calls=%fused_computation.38 | convolution fusion | flops 8388620 | bytes 12582931 | tf_op jit(solution)/shard_map/jk,kdc->jdc/dot_general | solution.py:62
  398.7 13.1 %copy.27 = f32[2,1024,1024]{1,2,0:T(8,128)} copy(f32[2,1024,1024]{2,0,1:T(2,128)} %fusion.9) | data formatting | bytes 16777216 | tf_op jit(solution)/shard_map/jk,kdc->jdc/dot_general | solution.py:62
  411.8 0.0 collective-permute-done.1
  411.8 11.3 %copy.23 = bf16[2,1024,1024]{2,0,1:T(2,128)(2,1)} copy(bf16[2,1024,1024]{1,2,0:T(8,128)(2,1)} %collective-permute-done.1) | data formatting | bytes 8388608 | tf_op jit(solution)/shard_map/ppermute | solution.py:9
  423.2 8.6 %fusion.8 = f32[2,1024,1024]{2,0,1:T(2,128)} fusion(bf16[2,1024,1024]{2,0,1:T(2,128)(2,1)} %copy.23, pred[]{:T(512)S(6)} %and.59, pred[2]{0:T(512)(128)(4,1)S(1)} %get-tuple-element.10, s32[2]{0:T(128)S(1)} %and_select_fusion.1, s32[2]{0:T(128)S(1)} %get-tuple-element.11), kind=kOutput, calls=%fused_computation.37 | convolution fusion | flops 8388620 | bytes 12582931 | tf_op jit(solution)/shard_map/jk,kdc->jdc/dot_general | solution.py:62
  431.8 13.2 %copy.25 = f32[2,1024,1024]{1,2,0:T(8,128)} copy(f32[2,1024,1024]{2,0,1:T(2,128)} %fusion.8) | data formatting | bytes 16777216 | tf_op jit(solution)/shard_map/jk,kdc->jdc/dot_general | solution.py:62
  444.9 0.0 collective-permute-done
  444.9 11.3 %copy.22 = bf16[2,1024,1024]{2,0,1:T(2,128)(2,1)} copy(bf16[2,1024,1024]{1,2,0:T(8,128)(2,1)} %collective-permute-done) | data formatting | bytes 8388608 | tf_op jit(solution)/shard_map/ppermute | solution.py:9
  456.2 8.7 %fusion.7 = f32[2,1024,1024]{2,0,1:T(2,128)} fusion(bf16[2,1024,1024]{2,0,1:T(2,128)(2,1)} %copy.22, pred[]{:T(512)S(6)} %and.55, pred[2]{0:T(512)(128)(4,1)S(1)} %get-tuple-element.10, s32[2]{0:T(128)S(1)} %and_select_fusion.2, s32[2]{0:T(128)S(1)} %get-tuple-element.11), kind=kOutput, calls=%fused_computation.36 | convolution fusion | flops 8388620 | bytes 12582931 | tf_op jit(solution)/shard_map/jk,kdc->jdc/dot_general | solution.py:62
  464.9 13.2 %copy.24 = f32[2,1024,1024]{1,2,0:T(8,128)} copy(f32[2,1024,1024]{2,0,1:T(2,128)} %fusion.7) | data formatting | bytes 16777216 | tf_op jit(solution)/shard_map/jk,kdc->jdc/dot_general | solution.py:62
  478.1 13.4 %fusion.1 = bf16[2,1024,1024]{1,2,0:T(8,128)(2,1)} fusion(f32[2,1024,1024]{1,2,0:T(8,128)} %copy.27, f32[2,1024,1024]{1,2,0:T(8,128)} %copy.24, f32[2,1024,1024]{1,2,0:T(8,128)} %copy.25, bf16[2,2048,1024]{2,1,0:T(8,128)(2,1)} %copy-done, s32[]{:T(128)S(6)} %select_n.73, pred[2]{0:T(512)(128)(4,1)S(1)} %get-tuple-element.10), kind=kLoop, calls=%fused_computation.5 | loop fusion | flops 12582912 | bytes 33554440 | tf_op jit(solution)/shard_map/convert_element_type | solution.py:67
  491.4 6.2 %copy.28 = bf16[2,1024,1024]{2,1,0:T(8,128)(2,1)} copy(bf16[2,1024,1024]{1,2,0:T(8,128)(2,1)} %fusion.1) | data formatting | bytes 8388608 | tf_op jit(solution)/shard_map/convert_element_type | solution.py:67
  (11 shorter events, 0.1 us)
Async XLA Ops:
  6.5 74.7 %all-gather.2.cloned.1.call-start = ((), (), s32[]{:S(2)}) async-start(), calls=%async_computation | async-start | bytes 14155776 | tf_op jit(solution)/shard_map/all_gather | solution.py:46
  98.9 3.2 copy-start
  102.1 6.5 %copy-start.1 = (s32[2,12]{1,0:T(2,128)S(1)}, s32[2,12]{1,0:T(2,128)}, u32[]{:S(2)}) copy-start(s32[2,12]{1,0:T(2,128)} %param.8) | copy-start | bytes 292
  104.6 274.0 %collective-permute-start.2 = (bf16[2,1024,1024]{1,2,0:T(8,128)(2,1)}, bf16[2,1024,1024]{1,2,0:T(8,128)(2,1)}, u32[]{:S(2)}, u32[]{:S(2)}) collective-permute-start(bf16[2,1024,1024]{1,2,0:T(8,128)(2,1)} %dynamic-slice_bitcast_fusion), channel_id=1, source_target_pairs={{0,72},{8,80},{16,88},{24,96},{32,104},{40,112},{48,120},{56,0},{6... | collective-permute-start | bytes 12582920 | tf_op jit(solution)/shard_map/ppermute | solution.py:9
  106.0 305.8 %collective-permute-start.1 = (bf16[2,1024,1024]{1,2,0:T(8,128)(2,1)}, bf16[2,1024,1024]{1,2,0:T(8,128)(2,1)}, u32[]{:S(2)}, u32[]{:S(2)}) collective-permute-start(bf16[2,1024,1024]{1,2,0:T(8,128)(2,1)} %dynamic-slice_bitcast_fusion), channel_id=1, source_target_pairs={{0,64},{8,72},{16,80},{24,88},{32,96},{40,104},{48,112},{56,120},{... | collective-permute-start | bytes 12582920 | tf_op jit(solution)/shard_map/ppermute | solution.py:9
  108.4 336.5 %collective-permute-start = (bf16[2,1024,1024]{1,2,0:T(8,128)(2,1)}, bf16[2,1024,1024]{1,2,0:T(8,128)(2,1)}, u32[]{:S(2)}, u32[]{:S(2)}) collective-permute-start(bf16[2,1024,1024]{1,2,0:T(8,128)(2,1)} %dynamic-slice_bitcast_fusion), channel_id=1, source_target_pairs={{0,56},{8,64},{16,72},{24,80},{32,88},{40,96},{48,104},{56,112},{6... | collective-permute-start | bytes 12582920 | tf_op jit(solution)/shard_map/ppermute | solution.py:9
Sparse Core Ops, SparseCore 0:
  11.5 69.6 all-gather.1
where the time goes:
time: 507 us; the launch traced here: 504 us
  waiting for transfers between devices  337 us (66%)
  local copies, waits for them, and re-layouts  90.3 us (18%)
  matrix products  43.7 us (9%)
  other arithmetic  15.7 us (3%)
  between operations  13.5 us (3%)
    ppermute x3, waiting for transfers between devices, from_behind(): lax.ppermute(array, axis, [(i, (i + by) % size) for i in range(size)])  267 us
    all_gather x1, waiting for transfers between devices, shards(): lax.all_gather(kv_rows, 'tp', axis=2, tiled=True)  69.8 us
    dot_general x3, local copies, waits for them, and re-layouts, shards(): jnp.einsum('jk,kdc->jdc', matches.astype(jnp.bfloat16), arrived, preferre...  39.5 us
    ppermute x3, local copies, waits for them, and re-layouts, from_behind(): lax.ppermute(array, axis, [(i, (i + by) % size) for i in range(size)])  34 us
    dot_general x3, matrix products, shards(): jnp.einsum('jk,kdc->jdc', matches.astype(jnp.bfloat16), arrived, preferre...  26 us
    dot_general x1, matrix products, shards(): jnp.einsum('std,stc->sdc', inputs, lax.all_gather(kv_rows, 'tp', axis=2,...  17.7 us
    convert_element_type x1, other arithmetic, shards(): return jnp.where(valid, summed, jnp.zeros_like(summed)).astype(jnp.bfloat16)  13.4 us
  transfers between devices with their start and end apart: 4, of which 2 were waited for; matrix products, arithmetic and copies ran while one was open for 14% of the time, Pallas kernels for 0%

commit v1 on v0

v1 whole, which is shorter than its diff:
```python
import functools

import jax
import jax.numpy as jnp
from jax import lax
from jax.experimental import pallas as pl
from jax.experimental.pallas import tpu as pltpu
from jax.sharding import PartitionSpec as P

MIB = 1 << 20
SETS = 2


def tied(*values):
    return lax.optimization_barrier(values)


def turn_kernel(pick, x_ref, o_ref):
    tile = x_ref.shape[1]
    rows = pl.program_id(1) * tile + lax.broadcasted_iota(jnp.int32, (tile, 1), 0)
    x = jnp.where(rows < pick[2], x_ref[0].astype(jnp.float32), 0.0)
    o_ref[0] = x.T.astype(o_ref.dtype)


def turn(pick, acts):
    slots, tokens, feats = acts.shape
    tile = 256
    return pl.pallas_call(
        turn_kernel,
        grid_spec=pltpu.PrefetchScalarGridSpec(
            num_scalar_prefetch=1,
            grid=(slots, tokens // tile),
            in_specs=[pl.BlockSpec((1, tile, feats), lambda s, i, p: (p[s], i, 0))],
            out_specs=pl.BlockSpec((1, feats, tile), lambda s, i, p: (s, 0, i)),
        ),
        out_shape=jax.ShapeDtypeStruct((slots, feats, tokens), acts.dtype),
        compiler_params=pltpu.CompilerParams(vmem_limit_bytes=24 * MIB),
        cost_estimate=pl.CostEstimate(flops=0, bytes_accessed=4 * acts.size, transcendentals=0),
    )(pick, acts)


def product(x_ref, kv_ref):
    kv = jnp.concatenate([kv_ref[t, 0] for t in range(kv_ref.shape[0])], axis=1)
    return jnp.dot(x_ref[0], kv, preferred_element_type=jnp.float32)


def send_kernel(pick, x_ref, kv_ref, o_ref):
    o_ref[...] = product(x_ref, kv_ref).astype(o_ref.dtype)


def send_block(pick, turned, kv):
    _, feats, tokens = turned.shape
    sources, _, _, width = kv.shape
    tile = 256
    out = (feats // 2, sources // 2 * width)
    return pl.pallas_call(
        send_kernel,
        grid_spec=pltpu.PrefetchScalarGridSpec(
            num_scalar_prefetch=1,
            grid=(out[0] // tile,),
            in_specs=[
                pl.BlockSpec((1, tile, tokens), lambda i, p: (p[0], p[1] * (out[0] // tile) + i, 0)),
                pl.BlockSpec((sources // 2, 1, tokens, width), lambda i, p: (p[3], p[2], 0, 0)),
            ],
            out_specs=pl.BlockSpec((tile, out[1]), lambda i, p: (i, 0)),
        ),
        out_shape=jax.ShapeDtypeStruct(out, turned.dtype),
        compiler_params=pltpu.CompilerParams(vmem_limit_bytes=24 * MIB),
        cost_estimate=pl.CostEstimate(
            flops=2 * out[0] * out[1] * tokens,
            bytes_accessed=2 * (out[0] * tokens + tokens * out[1] + out[0] * out[1]),
            transcendentals=0,
        ),
    )(pick, turned, kv)


def own_kernel(pick, x_ref, kv_ref, o_ref):
    o_ref[0] = product(x_ref, kv_ref).astype(o_ref.dtype)


def own_block(pick, turned, kv):
    slots, feats, tokens = turned.shape
    sources, _, _, width = kv.shape
    tile = 256
    cols = sources // 2 * width
    return pl.pallas_call(
        own_kernel,
        grid_spec=pltpu.PrefetchScalarGridSpec(
            num_scalar_prefetch=1,
            grid=(slots, feats // tile),
            in_specs=[
                pl.BlockSpec((1, tile, tokens), lambda s, i, p: (s, i, 0)),
                pl.BlockSpec((sources // 2, 1, tokens, width), lambda s, i, p: (p[2], p[s], 0, 0)),
            ],
            out_specs=pl.BlockSpec((1, tile, cols), lambda s, i, p: (s, i, 0)),
        ),
        out_shape=jax.ShapeDtypeStruct((slots, feats, cols), turned.dtype),
        compiler_params=pltpu.CompilerParams(vmem_limit_bytes=24 * MIB),
        cost_estimate=pl.CostEstimate(
            flops=2 * slots * feats * cols * tokens,
            bytes_accessed=2 * slots * (feats * tokens + tokens * cols + feats * cols),
            transcendentals=0,
        ),
    )(pick, turned, kv)


def join_kernel(width, pick, *refs):
    own, arrived, o_ref = refs[:SETS], refs[SETS:-1], refs[-1]
    code = pick[2 + pl.program_id(0) * 2 + pl.program_id(1)]
    count = len(arrived) // SETS
    span = SETS * width

    @pl.when(code == count)
    def _():
        o_ref[...] = jnp.zeros_like(o_ref)

    for choice in range(count):

        @pl.when(code == choice)
        def _():
            for c in range(SETS):
                total = own[c][0].astype(jnp.float32) + arrived[c * count + choice][...].astype(jnp.float32)
                total = total.astype(o_ref.dtype)
                for t in range(total.shape[1] // width):
                    o_ref[0, :, t * span + c * width : t * span + (c + 1) * width] = total[:, t * width : (t + 1) * width]


def join(pick, own, arrived, width):
    slots, feats, cols = own[0].shape
    half = feats // 2
    flat = [block for blocks in arrived for block in blocks]
    return pl.pallas_call(
        functools.partial(join_kernel, width),
        grid_spec=pltpu.PrefetchScalarGridSpec(
            num_scalar_prefetch=1,
            grid=(slots, 2),
            in_specs=[pl.BlockSpec((1, half, cols), lambda s, h, p: (p[s], h, 0))] * SETS
            + [pl.BlockSpec((half, cols), lambda s, h, p: (0, 0))] * len(flat),
            out_specs=pl.BlockSpec((1, half, SETS * cols), lambda s, h, p: (s, h, 0)),
        ),
        out_shape=jax.ShapeDtypeStruct((slots, feats, SETS * cols), own[0].dtype),
        compiler_params=pltpu.CompilerParams(vmem_limit_bytes=32 * MIB),
        cost_estimate=pl.CostEstimate(flops=0, bytes_accessed=14 * MIB, transcendentals=0),
    )(pick, *own, *flat)


def shards(acts, kv_grads, layer_section, token_counts):
    sections = lax.axis_size("section")
    pipe = lax.axis_index("pipe")
    section = lax.axis_index("section")
    acts, kv = acts[0], kv_grads[0]
    width = kv.shape[2] // SETS
    counts = jnp.sum((layer_section == section).astype(jnp.int32), axis=1)
    own_count = lax.dynamic_index_in_dim(counts, pipe, 0, keepdims=False)
    other_count = lax.dynamic_index_in_dim(counts, 1 - pipe, 0, keepdims=False)
    heavy = own_count == 2
    matched = own_count == other_count
    limit = lax.dynamic_index_in_dim(token_counts, pipe, 0, keepdims=False)
    h = heavy.astype(jnp.int32)
    f_slot = jnp.where(heavy, section % 2, 0)
    m_slot = 1 - f_slot

    def across(array):
        pairs = [
            (p * sections + s, (1 - p) * sections + (s ^ 1)) for p in range(2) for s in range(sections)
        ]
        return lax.ppermute(array, ("pipe", "section"), pairs)

    def beside(array):
        return lax.ppermute(array, "section", [(s, s ^ 1) for s in range(sections)])

    def scalars(*values):
        return jnp.stack([jnp.asarray(v, jnp.int32) for v in values])

    slot_of = lambda role: jnp.where(role == 1, m_slot, f_slot)
    other = 1 - pipe
    picks = [
        scalars(h, 0, slot_of(h), other),
        scalars(0, 1 - h, f_slot, other),
        scalars(1, 1, m_slot, other),
        scalars(0, 1, f_slot, other),
    ]
    gathered = []
    for c in range(SETS):
        part = kv[:, :, c * width : (c + 1) * width]
        if gathered:
            part, gathered[-1] = tied(part, gathered[-1])
        gathered.append(lax.all_gather(part, "tp", axis=0, tiled=False))
    turned = turn(scalars(f_slot, m_slot, limit), acts)
    own, arrived = [], []
    for c in range(SETS):
        kvs = gathered[c]
        sends = []
        for pick in picks:
            sends.append(send_block(pick, turned, kvs))
            turned, sends[-1] = tied(turned, sends[-1])
        c1, i1, x2, s2 = sends
        rc1, ri1, x2, s2 = tied(across(c1), beside(i1), x2, s2)
        c2, i2 = jnp.where(heavy, x2, ri1), jnp.where(heavy, s2, rc1)
        c2, i2, turned = tied(c2, i2, turned)
        rc2, ri2 = across(c2), beside(i2)
        own.append(own_block(scalars(f_slot, m_slot, pipe), turned, kvs))
        rc2, ri2, own[-1] = tied(rc2, ri2, own[-1])
        c3, i3 = jnp.where(heavy, ri1, ri2), jnp.where(heavy, rc1, rc2)
        if c + 1 < SETS:
            c3, i3, gathered[c + 1] = tied(c3, i3, gathered[c + 1])
        rc3, ri3 = across(c3), beside(i3)
        arrived.append((rc1, rc2, rc3, ri2, ri3))
    at_c1, at_c2, at_c3, at_i2, at_i3, none = range(6)
    fa = jnp.where(heavy == matched, at_c2, jnp.where(heavy, at_i2, at_i3))
    ma = jnp.where(heavy, jnp.where(matched, at_i2, at_c1), none)
    mb = jnp.where(heavy, jnp.where(matched, at_i3, at_c2), none)
    f_first = f_slot == 0
    codes = scalars(
        f_slot,
        m_slot,
        jnp.where(f_first, fa, ma),
        jnp.where(f_first, at_c3, mb),
        jnp.where(f_first, ma, fa),
        jnp.where(f_first, mb, at_c3),
    )
    return join(codes, own, arrived, width)


def solution(mesh):
    placed = (P("pipe", "section", None, "tp"), P("pipe", "section", None, "tp"), P(), P())
    return jax.shard_map(
        shards, mesh=mesh, in_specs=placed, out_specs=P("section", "tp", "pipe"), check_vma=False
    )
```

time: 507 us -> 176 us (0.35)
  waiting for transfers between devices: 337 us -> 85.9 us
  local copies, waits for them, and re-layouts: 90.3 us -> 20.4 us
  matrix products: 43.7 us -> 0 us
  Pallas kernels: 0 us -> 34.8 us
  other arithmetic: 15.7 us -> 4.93 us
  starting transfers between devices: 4.05 us -> 12.8 us
    ppermute x3 -> x12, waiting for transfers between devices: 267 us -> 42.5 us  [the longest x6 37.7 us: across(): return lax.ppermute(array, ('pipe', 'section'), pairs)]
    dot_general x4 -> x0, matrix products: 43.7 us -> none  [the longest x3 26 us: shards(): jnp.einsum('jk,kdc->jdc', matches.astype(jnp.bfloat16), arrived, preferre...]
    dot_general x3 -> x0, local copies, waits for them, and re-layouts: 39.5 us -> none  [shards(): jnp.einsum('jk,kdc->jdc', matches.astype(jnp.bfloat16), arrived, preferre...]
    pallas_call x0 -> x12, Pallas kernels: none -> 34.8 us  [the longest x8 14.8 us: send_block(): pl.pallas_call(send_kernel, grid_spec=pltpu.PrefetchScalarGridSpec(num_sc...]
    ppermute x3 -> x0, local copies, waits for them, and re-layouts: 34 us -> none  [from_behind(): lax.ppermute(array, axis, [(i, (i + by) % size) for i in range(size)])]
    all_gather x1 -> x2, waiting for transfers between devices: 69.8 us -> 43.3 us  [shards(): gathered.append(lax.all_gather(part, 'tp', axis=0, tiled=False))]
    convert_element_type x1 -> x0, other arithmetic: 13.4 us -> none  [shards(): return jnp.where(valid, summed, jnp.zeros_like(summed)).astype(jnp.bfloat16)]
    unnamed x5 -> x40, local copies, waits for them, and re-layouts: 4.93 us -> 16.4 us
  transfers between devices with their start and end apart: 4 -> 14, of which waited for: 2 -> 12; matrix products, arithmetic and copies ran while one was open for 14% -> 4% of each run, Pallas kernels for 0% -> 16%
where the time goes in v1:
time: 176 us; the launch traced here: 174 us
  waiting for transfers between devices  85.9 us (49%)
  Pallas kernels  34.8 us (20%)
  local copies, waits for them, and re-layouts  20.4 us (12%)
  between operations  15.6 us (9%)
  starting transfers between devices  12.8 us (7%)
  other arithmetic  4.93 us (3%)
    all_gather x2, waiting for transfers between devices, shards(): gathered.append(lax.all_gather(part, 'tp', axis=0, tiled=False))  43.3 us
    ppermute x6, waiting for transfers between devices, across(): return lax.ppermute(array, ('pipe', 'section'), pairs)  37.7 us
    unnamed x40, local copies, waits for them, and re-layouts  16.4 us
    pallas_call x8, Pallas kernels, send_block(): pl.pallas_call(send_kernel, grid_spec=pltpu.PrefetchScalarGridSpec(num_sc...  14.8 us
    pallas_call x2, Pallas kernels, own_block(): pl.pallas_call(own_kernel, grid_spec=pltpu.PrefetchScalarGridSpec(num_sca...  11.1 us
    ppermute x6, starting transfers between devices, across(): return lax.ppermute(array, ('pipe', 'section'), pairs)  10.2 us
    pallas_call x1, Pallas kernels, join(): pl.pallas_call(functools.partial(join_kernel, width), grid_spec=pltpu.Pre...  5.21 us
    ppermute x6, waiting for transfers between devices, beside(): return lax.ppermute(array, 'section', [(s, s ^ 1) for s in range(sections)])  4.78 us
  transfers between devices with their start and end apart: 14, of which 12 were waited for; matrix products, arithmetic and copies ran while one was open for 4% of the time, Pallas kernels for 16%

profile of v1, /device:TPU:24, one launch (start us, length us, event | category | flops | bytes accessed | tf_op | source)
XLA Modules:
  0.0 174.4 jit_solution(11996083628652313882)
XLA Ops:
  6.5 2.7 %fusion.5 = (bf16[2,1536,128]{2,1,0:T(8,128)(2,1)}, bf16[2,1536,128]{2,1,0:T(8,128)(2,1)}) fusion(bf16[2,1536,256]{2,1,0:T(8,128)(2,1)} %bitcast.32), kind=kLoop, calls=%fused_computation.21 | loop fusion | bytes 3145728 | tf_op jit(solution)/shard_map/slice | solution.py:185
  9.3 43.3 %all-gather.5.cloned.1.call-done = bf16[16,1536,128]{2,1,0:T(8,128)(2,1)} async-done(((bf16[2,1536,128]{2,1,0:T(8,128)(2,1)}), bf16[16,1536,128]{2,1,0:T(8,128)(2,1)}) %all-gather.5.cloned.1.call-update) | async-done | bytes 6291472 | tf_op jit(solution)/shard_map/all_gather | solution.py:188
  52.8 0.7 fusion.6
  54.2 0.6 dynamic_slice.12
  54.8 0.7 pad_add_fusion.2.pick
  55.5 2.9 %copy-done.5 = bf16[1,2,1536,1024]{3,2,1,0:T(8,128)(2,1)S(1)} copy-done((bf16[1,2,1536,1024]{3,2,1,0:T(8,128)(2,1)S(1)}, bf16[1,2,1536,1024]{3,2,1,0:T(8,128)(2,1)}, u32[]{:S(2)}) %copy-start.5) | copy-done | bytes 6291480
  58.4 3.7 %shard_map.46.x_ref = bf16[2,1024,1536]{2,1,0:T(8,128)(2,1)S(1)} custom-call(s32[3]{0:T(128)S(1)} %pad_add_fusion.2.pick, bf16[2,1536,1024]{2,1,0:T(8,128)(2,1)S(1)} %bitcast.31), custom_call_target="tpu_custom_call" | custom-call | bytes 12582912 | tf_op jit(solution)/shard_map/pallas_call | solution.py:28
  62.3 1.9 %shard_map.47 = bf16[512,512]{1,0:T(8,128)(2,1)S(1)} custom-call(s32[4]{0:T(128)S(1)} %get-tuple-element.93.pick, bf16[2,1024,1536]{2,1,0:T(8,128)(2,1)S(1)} %shard_map.46.x_ref, bf16[8,2,1536,128]{3,2,1,0:T(8,128)(2,1)S(1)} %bitcast.26), custom_call_target="tpu_custom_call" | custom-call | flops 805306368 | bytes 3670016 | tf_op jit(solution)/shard_map/pallas_call | solution.py:56
  64.1 0.6 collective-permute-start
  64.7 1.8 %shard_map.48 = bf16[512,512]{1,0:T(8,128)(2,1)S(1)} custom-call(s32[4]{0:T(128)S(1)} %get-tuple-element.91.pick, bf16[2,1024,1536]{2,1,0:T(8,128)(2,1)S(1)} %shard_map.46.x_ref, bf16[8,2,1536,128]{3,2,1,0:T(8,128)(2,1)S(1)} %bitcast.27), custom_call_target="tpu_custom_call" | custom-call | flops 805306368 | bytes 3670016 | tf_op jit(solution)/shard_map/pallas_call | solution.py:56
  66.6 1.0 collective-permute-start.1
  67.5 1.8 %shard_map.49 = bf16[512,512]{1,0:T(8,128)(2,1)S(1)} custom-call(s32[4]{0:T(128)S(1)} %get-tuple-element.94.pick, bf16[2,1024,1536]{2,1,0:T(8,128)(2,1)S(1)} %shard_map.46.x_ref, bf16[8,2,1536,128]{3,2,1,0:T(8,128)(2,1)S(1)} %bitcast.28), custom_call_target="tpu_custom_call" | custom-call | flops 805306368 | bytes 3670016 | tf_op jit(solution)/shard_map/pallas_call | solution.py:56
  69.4 1.8 %shard_map.50 = bf16[512,512]{1,0:T(8,128)(2,1)S(1)} custom-call(s32[4]{0:T(128)S(1)} %get-tuple-element.92.pick, bf16[2,1024,1536]{2,1,0:T(8,128)(2,1)S(1)} %shard_map.46.x_ref, bf16[8,2,1536,128]{3,2,1,0:T(8,128)(2,1)S(1)} %bitcast.29), custom_call_target="tpu_custom_call" | custom-call | flops 805306368 | bytes 3670016 | tf_op jit(solution)/shard_map/pallas_call | solution.py:56
  71.2 8.3 %collective-permute-done.refs_2_ = bf16[512,512]{1,0:T(8,128)(2,1)S(1)} collective-permute-done((bf16[512,512]{1,0:T(8,128)(2,1)S(1)}, bf16[512,512]{1,0:T(8,128)(2,1)S(1)}, u32[]{:S(2)}, u32[]{:S(2)}) %collective-permute-start) | collective-permute-done | bytes 524320 | tf_op jit(solution)/shard_map/ppermute | solution.py:167
  79.5 0.9 collective-permute-done.1
  80.6 2.8 %collective-permute-start.2 = (bf16[512,512]{1,0:T(8,128)(2,1)S(1)}, bf16[512,512]{1,0:T(8,128)(2,1)S(1)}, u32[]{:S(2)}, u32[]{:S(2)}) collective-permute-start(bf16[512,512]{1,0:T(8,128)(2,1)S(1)} %broadcast_select_fusion.7), channel_id=1, source_target_pairs={{0,72},{8,64},{16,88},{24,80},{32,104},{40,96},{48,120},{56,112},{... | collective-permute-start | bytes 1572872 | tf_op jit(solution)/shard_map/ppermute | solution.py:167
  83.5 5.6 %shard_map.51.refs_0_ = bf16[2,1024,512]{2,1,0:T(8,128)(2,1)S(1)} custom-call(s32[3]{0:T(128)S(1)} %pad_add_fusion.4.pick, bf16[2,1024,1536]{2,1,0:T(8,128)(2,1)S(1)} %shard_map.46.x_ref, bf16[8,2,1536,128]{3,2,1,0:T(8,128)(2,1)S(1)} %bitcast.30), custom_call_target="tpu_custom_call" | custom-call | flops 3221225472 | bytes 11534336 | tf_op jit(solution)/shard_map/pallas_call | solution.py:86
  89.1 5.8 %collective-permute-done.2.refs_3_ = bf16[512,512]{1,0:T(8,128)(2,1)S(1)} collective-permute-done((bf16[512,512]{1,0:T(8,128)(2,1)S(1)}, bf16[512,512]{1,0:T(8,128)(2,1)S(1)}, u32[]{:S(2)}, u32[]{:S(2)}) %collective-permute-start.2) | collective-permute-done | bytes 524320 | tf_op jit(solution)/shard_map/ppermute | solution.py:167
  94.9 1.3 collective-permute-done.3.refs_5_
  96.2 0.9 broadcast_select_fusion.5
  97.1 0.8 copy-done.8
  97.9 0.9 broadcast_select_fusion.4
  98.7 2.8 %copy-done.1 = bf16[2,1024,1536]{2,1,0:T(8,128)(2,1)S(1)} copy-done((bf16[2,1024,1536]{2,1,0:T(8,128)(2,1)S(1)}, bf16[2,1024,1536]{2,1,0:T(8,128)(2,1)}, u32[]{:S(2)}) %copy-start.1) | copy-done | bytes 6291480
  101.5 2.8 %copy-done.2 = bf16[16,1536,128]{2,1,0:T(8,128)(2,1)S(1)} copy-done((bf16[16,1536,128]{2,1,0:T(8,128)(2,1)S(1)}, bf16[16,1536,128]{2,1,0:T(8,128)(2,1)}, u32[]{:S(2)}) %copy-start.2) | copy-done | bytes 6291480
  104.3 1.8 %shard_map.52 = bf16[512,512]{1,0:T(8,128)(2,1)S(1)} custom-call(s32[4]{0:T(128)S(1)} %get-tuple-element.93.pick, bf16[2,1024,1536]{2,1,0:T(8,128)(2,1)S(1)} %copy-done.1, bf16[8,2,1536,128]{3,2,1,0:T(8,128)(2,1)S(1)} %bitcast.17), custom_call_target="tpu_custom_call" | custom-call | flops 805306368 | bytes 3670016 | tf_op jit(solution)/shard_map/pallas_call | solution.py:56
  106.2 1.7 collective-permute-start.4
  107.9 1.8 %shard_map.53 = bf16[512,512]{1,0:T(8,128)(2,1)S(1)} custom-call(s32[4]{0:T(128)S(1)} %get-tuple-element.91.pick, bf16[2,1024,1536]{2,1,0:T(8,128)(2,1)S(1)} %copy-done.1, bf16[8,2,1536,128]{3,2,1,0:T(8,128)(2,1)S(1)} %bitcast.18), custom_call_target="tpu_custom_call" | custom-call | flops 805306368 | bytes 3670016 | tf_op jit(solution)/shard_map/pallas_call | solution.py:56
  109.8 1.8 %shard_map.54 = bf16[512,512]{1,0:T(8,128)(2,1)S(1)} custom-call(s32[4]{0:T(128)S(1)} %get-tuple-element.94.pick, bf16[2,1024,1536]{2,1,0:T(8,128)(2,1)S(1)} %copy-done.1, bf16[8,2,1536,128]{3,2,1,0:T(8,128)(2,1)S(1)} %bitcast.19), custom_call_target="tpu_custom_call" | custom-call | flops 805306368 | bytes 3670016 | tf_op jit(solution)/shard_map/pallas_call | solution.py:56
  111.7 1.8 %shard_map.55 = bf16[512,512]{1,0:T(8,128)(2,1)S(1)} custom-call(s32[4]{0:T(128)S(1)} %get-tuple-element.92.pick, bf16[2,1024,1536]{2,1,0:T(8,128)(2,1)S(1)} %copy-done.1, bf16[8,2,1536,128]{3,2,1,0:T(8,128)(2,1)S(1)} %bitcast.20), custom_call_target="tpu_custom_call" | custom-call | flops 805306368 | bytes 3670016 | tf_op jit(solution)/shard_map/pallas_call | solution.py:56
  113.5 5.8 %collective-permute-done.4.refs_7_ = bf16[512,512]{1,0:T(8,128)(2,1)S(1)} collective-permute-done((bf16[512,512]{1,0:T(8,128)(2,1)S(1)}, bf16[512,512]{1,0:T(8,128)(2,1)S(1)}, u32[]{:S(2)}, u32[]{:S(2)}) %collective-permute-start.4) | collective-permute-done | bytes 524320 | tf_op jit(solution)/shard_map/ppermute | solution.py:167
  119.3 2.3 %collective-permute-done.5 = bf16[512,512]{1,0:T(8,128)(2,1)S(1)} collective-permute-done((bf16[512,512]{1,0:T(8,128)(2,1)S(1)}, bf16[512,512]{1,0:T(8,128)(2,1)S(1)}, u32[]{:S(2)}, u32[]{:S(2)}) %collective-permute-start.5) | collective-permute-done | bytes 524320 | tf_op jit(solution)/shard_map/ppermute | solution.py:170
  121.8 1.4 collective-permute-start.6
  123.2 1.9 %collective-permute-start.8 = (bf16[512,512]{1,0:T(8,128)(2,1)}, bf16[512,512]{1,0:T(8,128)(2,1)}, u32[]{:S(2)}, u32[]{:S(2)}) collective-permute-start(bf16[512,512]{1,0:T(8,128)(2,1)} %broadcast_select_fusion.5), channel_id=1, source_target_pairs={{0,72},{8,64},{16,88},{24,80},{32,104},{40,96},{48,120},{56,112},{... | collective-permute-start | bytes 1572872 | tf_op jit(solution)/shard_map/ppermute | solution.py:167
  125.1 1.4 collective-permute-start.9
  126.5 5.5 %shard_map.56.refs_1_ = bf16[2,1024,512]{2,1,0:T(8,128)(2,1)S(1)} custom-call(s32[3]{0:T(128)S(1)} %pad_add_fusion.4.pick, bf16[2,1024,1536]{2,1,0:T(8,128)(2,1)S(1)} %copy-done.1, bf16[8,2,1536,128]{3,2,1,0:T(8,128)(2,1)S(1)} %bitcast.23), custom_call_target="tpu_custom_call" | custom-call | flops 3221225472 | bytes 11534336 | tf_op jit(solution)/shard_map/pallas_call | solution.py:86
  132.1 1.3 copy-done.3
  133.4 4.5 %collective-permute-done.6.refs_8_ = bf16[512,512]{1,0:T(8,128)(2,1)S(1)} collective-permute-done((bf16[512,512]{1,0:T(8,128)(2,1)S(1)}, bf16[512,512]{1,0:T(8,128)(2,1)S(1)}, u32[]{:S(2)}, u32[]{:S(2)}) %collective-permute-start.6) | collective-permute-done | bytes 524320 | tf_op jit(solution)/shard_map/ppermute | solution.py:167
  138.0 1.0 broadcast_select_fusion.1
  139.0 1.8 %collective-permute-start.10 = (bf16[512,512]{1,0:T(8,128)(2,1)}, bf16[512,512]{1,0:T(8,128)(2,1)}, u32[]{:S(2)}, u32[]{:S(2)}) collective-permute-start(bf16[512,512]{1,0:T(8,128)(2,1)} %broadcast_select_fusion.1), channel_id=1, source_target_pairs={{0,72},{8,64},{16,88},{24,80},{32,104},{40,96},{48,120},{56,112},{... | collective-permute-start | bytes 1572872 | tf_op jit(solution)/shard_map/ppermute | solution.py:167
  140.9 0.9 broadcast_select_fusion
  143.2 6.1 %collective-permute-done.8.refs_4_ = bf16[512,512]{1,0:T(8,128)(2,1)} collective-permute-done((bf16[512,512]{1,0:T(8,128)(2,1)}, bf16[512,512]{1,0:T(8,128)(2,1)}, u32[]{:S(2)}, u32[]{:S(2)}) %collective-permute-start.8) | collective-permute-done | bytes 524320 | tf_op jit(solution)/shard_map/ppermute | solution.py:167
  149.4 7.2 %collective-permute-done.10.refs_9_ = bf16[512,512]{1,0:T(8,128)(2,1)} collective-permute-done((bf16[512,512]{1,0:T(8,128)(2,1)}, bf16[512,512]{1,0:T(8,128)(2,1)}, u32[]{:S(2)}, u32[]{:S(2)}) %collective-permute-start.10) | collective-permute-done | bytes 524320 | tf_op jit(solution)/shard_map/ppermute | solution.py:167
  156.6 1.6 copy-done.4
  158.2 1.0 copy-done.7
  159.2 1.0 copy-done.9
  160.3 1.0 copy-done.11
  161.3 1.0 copy-done.13
  162.3 5.2 %shard_map.57 = bf16[2,1024,1024]{2,1,0:T(8,128)(2,1)} custom-call(s32[6]{0:T(128)S(1)} %stack.75.pick, bf16[2,1024,512]{2,1,0:T(8,128)(2,1)S(1)} %shard_map.51.refs_0_, bf16[2,1024,512]{2,1,0:T(8,128)(2,1)S(1)} %copy-done.4, bf16[512,512]{1,0:T(8,128)(2,1)S(1)} %collective-permute-done.refs_2_, bf16[512,512]{1,0:T(8,128)(2,1)S(1)} %copy-done.7, ...), custom_call_target="tpu_custom_call" | custom-call | bytes 14680064 | tf_op jit(solution)/shard_map/pallas_call | solution.py:132
  (54 shorter events, 1.1 us)
Async XLA Ops:
  6.5 46.1 %copy-start.14 = (s32[2,12]{1,0:T(2,128)S(1)}, s32[2,12]{1,0:T(2,128)}, u32[]{:S(2)}) copy-start(s32[2,12]{1,0:T(2,128)} %param.6) | copy-start | bytes 292
  6.5 47.6 %copy-start.15 = (s32[2]{0:T(128)S(1)}, s32[2]{0:T(128)}, u32[]{:S(2)}) copy-start(s32[2]{0:T(128)} %param.7) | copy-start | bytes 28
  6.5 46.1 %all-gather.5.cloned.1.call-start = ((), (), s32[]{:S(2)}) async-start(), calls=%async_computation | async-start | bytes 7077888 | tf_op jit(solution)/shard_map/all_gather | solution.py:188
  9.2 89.5 %all-gather.7.cloned.1.call-start = ((), (), s32[]{:S(2)}) async-start(), calls=%async_computation.1 | async-start | bytes 7077888 | tf_op jit(solution)/shard_map/all_gather | solution.py:188
  55.5 6.8 %slice-start.2 = ((s8[6291456]{0:T(1024)(128)(4,1)}), s8[4194304]{0:T(1024)(128)(4,1)S(1)}, s32[]{:S(2)}) async-start(s8[6291456]{0:T(1024)(128)(4,1)} %bitcast.24), calls=%async_computation.4 | async-start | bytes 8388608
  55.5 2.9 %copy-start.5 = (bf16[1,2,1536,1024]{3,2,1,0:T(8,128)(2,1)S(1)}, bf16[1,2,1536,1024]{3,2,1,0:T(8,128)(2,1)}, u32[]{:S(2)}) copy-start(bf16[1,2,1536,1024]{3,2,1,0:T(8,128)(2,1)} %param.4) | copy-start | bytes 18874372
  58.4 3.8 %slice-start.3 = ((s8[6291456]{0:T(1024)(128)(4,1)}), s8[2097152]{0:T(1024)(128)(4,1)S(1)}, s32[]{:S(2)}) async-start(s8[6291456]{0:T(1024)(128)(4,1)} %bitcast.24), calls=%async_computation.5 | async-start | bytes 4194304
  62.1 21.4 %copy-start = (bf16[2,1024,1536]{2,1,0:T(8,128)(2,1)}, bf16[2,1024,1536]{2,1,0:T(8,128)(2,1)S(1)}, u32[]{:S(2)}) copy-start(bf16[2,1024,1536]{2,1,0:T(8,128)(2,1)S(1)} %shard_map.46.x_ref) | copy-start | bytes 18874372
  64.1 15.4 %collective-permute-start = (bf16[512,512]{1,0:T(8,128)(2,1)S(1)}, bf16[512,512]{1,0:T(8,128)(2,1)S(1)}, u32[]{:S(2)}, u32[]{:S(2)}) collective-permute-start(bf16[512,512]{1,0:T(8,128)(2,1)S(1)} %shard_map.47), channel_id=1, source_target_pairs={{0,72},{8,64},{16,88},{24,80},{32,104},{40,96},{48,120},{56,112},{... | collective-permute-start | bytes 1572872 | tf_op jit(solution)/shard_map/ppermute | solution.py:167
  66.6 13.9 %collective-permute-start.1 = (bf16[512,512]{1,0:T(8,128)(2,1)S(1)}, bf16[512,512]{1,0:T(8,128)(2,1)S(1)}, u32[]{:S(2)}, u32[]{:S(2)}) collective-permute-start(bf16[512,512]{1,0:T(8,128)(2,1)S(1)} %shard_map.48), channel_id=1, source_target_pairs={{0,8},{8,0},{16,24},{24,16},{32,40},{40,32},{48,56},{56,48},{1,9},... | collective-permute-start | bytes 1572872 | tf_op jit(solution)/shard_map/ppermute | solution.py:170
  80.6 14.3 %collective-permute-start.2 = (bf16[512,512]{1,0:T(8,128)(2,1)S(1)}, bf16[512,512]{1,0:T(8,128)(2,1)S(1)}, u32[]{:S(2)}, u32[]{:S(2)}) collective-permute-start(bf16[512,512]{1,0:T(8,128)(2,1)S(1)} %broadcast_select_fusion.7), channel_id=1, source_target_pairs={{0,72},{8,64},{16,88},{24,80},{32,104},{40,96},{48,120},{56,112},{... | collective-permute-start | bytes 1572872 | tf_op jit(solution)/shard_map/ppermute | solution.py:167
  83.4 12.8 %collective-permute-start.3 = (bf16[512,512]{1,0:T(8,128)(2,1)S(1)}, bf16[512,512]{1,0:T(8,128)(2,1)S(1)}, u32[]{:S(2)}, u32[]{:S(2)}) collective-permute-start(bf16[512,512]{1,0:T(8,128)(2,1)S(1)} %broadcast_select_fusion.6), channel_id=1, source_target_pairs={{0,8},{8,0},{16,24},{24,16},{32,40},{40,32},{48,56},{56,48},{1,9},... | collective-permute-start | bytes 1572872 | tf_op jit(solution)/shard_map/ppermute | solution.py:170
  94.9 2.1 %copy-start.6 = (bf16[512,512]{1,0:T(8,128)(2,1)}, bf16[512,512]{1,0:T(8,128)(2,1)S(1)}, u32[]{:S(2)}) copy-start(bf16[512,512]{1,0:T(8,128)(2,1)S(1)} %collective-permute-done.2.refs_3_) | copy-start | bytes 1572868
  97.1 0.8 copy-start.8
  98.7 2.8 %copy-start.1 = (bf16[2,1024,1536]{2,1,0:T(8,128)(2,1)S(1)}, bf16[2,1024,1536]{2,1,0:T(8,128)(2,1)}, u32[]{:S(2)}) copy-start(bf16[2,1024,1536]{2,1,0:T(8,128)(2,1)} %copy-done) | copy-start | bytes 18874372
  101.5 2.8 %copy-start.2 = (bf16[16,1536,128]{2,1,0:T(8,128)(2,1)S(1)}, bf16[16,1536,128]{2,1,0:T(8,128)(2,1)}, u32[]{:S(2)}) copy-start(bf16[16,1536,128]{2,1,0:T(8,128)(2,1)} %all-gather.7.cloned.1.call-done) | copy-start | bytes 18874372
  106.2 13.1 %collective-permute-start.4 = (bf16[512,512]{1,0:T(8,128)(2,1)S(1)}, bf16[512,512]{1,0:T(8,128)(2,1)S(1)}, u32[]{:S(2)}, u32[]{:S(2)}) collective-permute-start(bf16[512,512]{1,0:T(8,128)(2,1)S(1)} %shard_map.52), channel_id=1, source_target_pairs={{0,72},{8,64},{16,88},{24,80},{32,104},{40,96},{48,120},{56,112},{... | collective-permute-start | bytes 1572872 | tf_op jit(solution)/shard_map/ppermute | solution.py:167
  109.7 11.9 %collective-permute-start.5 = (bf16[512,512]{1,0:T(8,128)(2,1)S(1)}, bf16[512,512]{1,0:T(8,128)(2,1)S(1)}, u32[]{:S(2)}, u32[]{:S(2)}) collective-permute-start(bf16[512,512]{1,0:T(8,128)(2,1)S(1)} %shard_map.53), channel_id=1, source_target_pairs={{0,8},{8,0},{16,24},{24,16},{32,40},{40,32},{48,56},{56,48},{1,9},... | collective-permute-start | bytes 1572872 | tf_op jit(solution)/shard_map/ppermute | solution.py:170
  109.8 16.7 %slice-start = ((s8[6291456]{0:T(1024)(128)(4,1)}), s8[4194304]{0:T(1024)(128)(4,1)S(1)}, s32[]{:S(2)}) async-start(s8[6291456]{0:T(1024)(128)(4,1)} %bitcast.21), calls=%async_computation.2 | async-start | bytes 8388608
  111.7 14.9 %slice-start.1 = ((s8[6291456]{0:T(1024)(128)(4,1)}), s8[2097152]{0:T(1024)(128)(4,1)S(1)}, s32[]{:S(2)}) async-start(s8[6291456]{0:T(1024)(128)(4,1)} %bitcast.21), calls=%async_computation.3 | async-start | bytes 4194304
  121.8 16.2 %collective-permute-start.6 = (bf16[512,512]{1,0:T(8,128)(2,1)S(1)}, bf16[512,512]{1,0:T(8,128)(2,1)S(1)}, u32[]{:S(2)}, u32[]{:S(2)}) collective-permute-start(bf16[512,512]{1,0:T(8,128)(2,1)S(1)} %broadcast_select_fusion.3), channel_id=1, source_target_pairs={{0,72},{8,64},{16,88},{24,80},{32,104},{40,96},{48,120},{56,112},{... | collective-permute-start | bytes 1572872 | tf_op jit(solution)/shard_map/ppermute | solution.py:167
  123.2 14.9 %collective-permute-start.7 = (bf16[512,512]{1,0:T(8,128)(2,1)S(1)}, bf16[512,512]{1,0:T(8,128)(2,1)S(1)}, u32[]{:S(2)}, u32[]{:S(2)}) collective-permute-start(bf16[512,512]{1,0:T(8,128)(2,1)S(1)} %broadcast_select_fusion.2), channel_id=1, source_target_pairs={{0,8},{8,0},{16,24},{24,16},{32,40},{40,32},{48,56},{56,48},{1,9},... | collective-permute-start | bytes 1572872 | tf_op jit(solution)/shard_map/ppermute | solution.py:170
  123.2 26.1 %collective-permute-start.8 = (bf16[512,512]{1,0:T(8,128)(2,1)}, bf16[512,512]{1,0:T(8,128)(2,1)}, u32[]{:S(2)}, u32[]{:S(2)}) collective-permute-start(bf16[512,512]{1,0:T(8,128)(2,1)} %broadcast_select_fusion.5), channel_id=1, source_target_pairs={{0,72},{8,64},{16,88},{24,80},{32,104},{40,96},{48,120},{56,112},{... | collective-permute-start | bytes 1572872 | tf_op jit(solution)/shard_map/ppermute | solution.py:167
  125.1 24.3 %collective-permute-start.9 = (bf16[512,512]{1,0:T(8,128)(2,1)}, bf16[512,512]{1,0:T(8,128)(2,1)}, u32[]{:S(2)}, u32[]{:S(2)}) collective-permute-start(bf16[512,512]{1,0:T(8,128)(2,1)} %broadcast_select_fusion.4), channel_id=1, source_target_pairs={{0,8},{8,0},{16,24},{24,16},{32,40},{40,32},{48,56},{56,48},{1,9},... | collective-permute-start | bytes 1572872 | tf_op jit(solution)/shard_map/ppermute | solution.py:170
  132.1 1.3 copy-start.3
  137.9 3.0 %copy-start.10 = (bf16[512,512]{1,0:T(8,128)(2,1)}, bf16[512,512]{1,0:T(8,128)(2,1)S(1)}, u32[]{:S(2)}) copy-start(bf16[512,512]{1,0:T(8,128)(2,1)S(1)} %collective-permute-done.6.refs_8_) | copy-start | bytes 1572868
  138.0 3.7 %copy-start.12 = (bf16[512,512]{1,0:T(8,128)(2,1)}, bf16[512,512]{1,0:T(8,128)(2,1)S(1)}, u32[]{:S(2)}) copy-start(bf16[512,512]{1,0:T(8,128)(2,1)S(1)} %collective-permute-done.7.refs_10_) | copy-start | bytes 1572868
  139.0 17.5 %collective-permute-start.10 = (bf16[512,512]{1,0:T(8,128)(2,1)}, bf16[512,512]{1,0:T(8,128)(2,1)}, u32[]{:S(2)}, u32[]{:S(2)}) collective-permute-start(bf16[512,512]{1,0:T(8,128)(2,1)} %broadcast_select_fusion.1), channel_id=1, source_target_pairs={{0,72},{8,64},{16,88},{24,80},{32,104},{40,96},{48,120},{56,112},{... | collective-permute-start | bytes 1572872 | tf_op jit(solution)/shard_map/ppermute | solution.py:167
  141.8 14.8 %collective-permute-start.11 = (bf16[512,512]{1,0:T(8,128)(2,1)}, bf16[512,512]{1,0:T(8,128)(2,1)}, u32[]{:S(2)}, u32[]{:S(2)}) collective-permute-start(bf16[512,512]{1,0:T(8,128)(2,1)} %broadcast_select_fusion), channel_id=1, source_target_pairs={{0,8},{8,0},{16,24},{24,16},{32,40},{40,32},{48,56},{56,48},{1,9},... | collective-permute-start | bytes 1572872 | tf_op jit(solution)/shard_map/ppermute | solution.py:170
  156.6 1.6 copy-start.4
  158.2 1.0 copy-start.7
  159.2 1.0 copy-start.9
  160.3 1.0 copy-start.11
  161.3 1.0 copy-start.13
Sparse Core Ops, SparseCore 0:
  9.3 43.2 all-gather.4
  54.3 41.0 all-gather.6
